TPU v7x, 32 devices: a whole 2x2x4 slice. The times are simulated.
32 devices in a mesh: seq: 16 (over z, y, core), ch: 2 (over x).
Axes of the slice: x: 2, y: 2, z: 4, core: 2. Of those that a mesh axis runs over, the one named last changes fastest.
Arguments:
- tokens: int32 [4096], P('seq'), may hold values from 0 to 3
- feature_table: bfloat16 [512, 3, 4096], P(None, None, 'ch'), may hold values from -6 to 6
- short_filter: float32 [3, 7, 4096], P(None, None, 'ch'), may hold values from -2 to 2
- med_filter: bfloat16 [128, 256], P(None, 'ch'), may hold values from -0.5 to 0.5
- med_bias: float32 [4096], P('ch'), may hold values from 0.5 to 1.5
- out_weight: bfloat16 [4096, 4096], P('seq', 'ch'), may hold values from -0.09375 to 0.09375
Outputs:
- scored: bfloat16 [4096, 4096], P('seq', 'ch')
All inputs are finite; a program needn't handle non-finite values.
Results may differ from a plain program's by a relative error of at most 0.01.
Values may be sent and summed in bfloat16 or wider, within the bound.
A program may use at most 128 MiB of HBM per device.

v0:
```python
import jax
import jax.numpy as jnp
import numpy as np
from jax import lax
from jax.sharding import PartitionSpec as P

base_codes = np.array([65, 67, 71, 84], dtype=np.int32)


def from_behind(value, axis, steps):
    count = lax.axis_size(axis)
    initial, last = (max(0, -steps), min(count, count - steps))
    return lax.ppermute(value, axis, [(source, source + steps) for source in range(initial, last)])


def rims(forward_rows, reverse_rows, rim_width):
    start_row = forward_rows.shape[0] - rim_width
    forward = from_behind(forward_rows[start_row:], "seq", 1)
    second = from_behind(reverse_rows[start_row:], "seq", -1)
    return jnp.stack([forward, second])


def toeplitz(filters):
    tap_count = filters.shape[0]
    row_index = jnp.arange(tap_count, dtype=jnp.int32)[:, None]
    col_index = jnp.arange(2 * tap_count - 1, dtype=jnp.int32)[None, :]
    tap_index = row_index - col_index + tap_count - 1
    inside = (tap_index >= 0) & (tap_index < tap_count)
    picked = jnp.take(filters, jnp.clip(tap_index, 0, tap_count - 1), axis=0)
    toeplitz_table = jnp.where(inside[:, :, None], picked, jnp.zeros((), filters.dtype))
    return jnp.transpose(toeplitz_table, (2, 0, 1))


def per_device(tokens, feature_table, short_filter, med_filter, med_bias, out_weight):
    length = tokens.shape[0]
    width_local = feature_table.shape[2]
    short_taps = short_filter.shape[1]
    tap_count = med_filter.shape[0]
    groups_local = med_filter.shape[1]
    group_width = width_local // groups_local
    strand_bases = jnp.stack([tokens, 3 - jnp.flip(tokens, 0)])
    corner = feature_table[base_codes]
    features = jnp.take(corner, strand_bases, axis=0)
    short_rim = rims(features[0], features[1], short_taps - 1)
    extended = jnp.concatenate([short_rim, features], axis=1).astype(jnp.float32)
    short_out = jnp.zeros((2, length, 3, width_local), jnp.float32)
    for shift_index in range(short_taps):
        begin = short_taps - 1 - shift_index
        short_out = (
            short_out + short_filter[:, shift_index, :] * extended[:, begin : begin + length]
        )
    gated_mix = (short_out[:, :, 0] * short_out[:, :, 2]).astype(jnp.bfloat16)
    medium_rim = rims(gated_mix[0], gated_mix[1], tap_count - 1)
    padded = jnp.concatenate([medium_rim, gated_mix], axis=1)
    kernel = toeplitz(med_filter)
    block_count = length // tap_count
    windows = jnp.stack(
        [
            padded[:, block_index * tap_count : block_index * tap_count + 2 * tap_count - 1]
            for block_index in range(block_count)
        ],
        axis=1,
    )
    windows = windows.reshape(2, block_count, 2 * tap_count - 1, groups_local, group_width)
    medium = jnp.einsum("grw,snwgc->snrgc", kernel, windows, preferred_element_type=jnp.float32)
    medium = medium.reshape(2, length, width_local) + med_bias * gated_mix.astype(jnp.float32)
    hidden = (short_out[:, :, 1] * medium).astype(jnp.bfloat16)
    reverse = hidden[1]
    averaged = (
        0.5 * (hidden[0].astype(jnp.float32) + jnp.flip(reverse, 0).astype(jnp.float32))
    ).astype(jnp.bfloat16)
    gathered = lax.all_gather(averaged, "ch", axis=1, tiled=True)
    weight_rows = lax.all_gather(out_weight, "seq", axis=0, tiled=True)
    result = jnp.dot(gathered, weight_rows, preferred_element_type=jnp.float32)
    return result.astype(jnp.bfloat16)


def solution(mesh):
    placed = (
        P("seq"),
        P(None, None, "ch"),
        P(None, None, "ch"),
        P(None, "ch"),
        P("ch"),
        P("seq", "ch"),
    )
    return jax.shard_map(
        per_device, mesh=mesh, in_specs=placed, out_specs=P("seq", "ch"), check_vma=False
    )
```

profile of v0, /device:TPU:0, one launch (start us, length us, event | category | flops | bytes accessed | tf_op | source)
XLA Modules:
  0.0 461.9 jit_solution(11697910313658378829)
XLA Ops:
  6.5 0.0 all-gather.3.cloned.1.call-start
  6.5 0.7 pad_clamp_fusion.2
  7.2 1.6 gather_fusion
  8.8 0.8 rev.8
  9.6 0.7 compare_select_fusion.2
  10.3 17.1 %gather_fusion.1 = bf16[512,3,2048]{2,1,0:T(4,128)(2,1)} fusion(bf16[4,3,2048]{2,1,0:T(4,128)(2,1)S(1)} %copy.31, s32[1024]{0:T(1024)S(1)} %pad_clamp_fusion.1), kind=kCustom, calls=%fused_computation.1 | custom fusion | bytes 12584960 | tf_op jit(solution)/shard_map/jit(_take)/gather | solution.py:43
  27.4 13.0 %copy.32 = bf16[2,256,3,2048]{1,3,0,2:T(8,128)(2,1)} copy(bf16[2,256,3,2048]{3,2,1,0:T(4,128)(2,1)} %bitcast.65) | data formatting | bytes 12582912 | tf_op jit(solution)/shard_map/jit(_take)/gather | solution.py:43
  40.4 3.3 broadcast_select_fusion
  43.7 2.6 copy-done.2
  46.4 0.9 slice_bitcast_fusion.2
  47.3 0.7 copy.35
  48.0 1.3 collective-permute-start.1
  49.3 0.7 copy.33
  50.0 3.7 collective-permute-start
  53.8 0.1 fusion.23
  53.9 0.3 reshape.198
  54.3 65.9 %gather_fusion.2 = bf16[32640,128]{1,0:T(8,128)(2,1)} fusion(bf16[128,128]{1,0:T(8,128)(2,1)S(1)} %copy-done, s32[32768]{0:T(1024)S(1)} %pad_clamp_fusion), kind=kCustom, calls=%fused_computation.2 | custom fusion | bytes 16842240 | tf_op jit(solution)/shard_map/jit(_take)/gather | solution.py:29
  120.2 9.7 %reshape.197 = bf16[128,255,128]{2,1,0:T(8,128)(2,1)} reshape(bf16[32640,128]{1,0:T(8,128)(2,1)} %gather_fusion.2) | data formatting | bytes 16711680 | tf_op jit(solution)/shard_map/jit(_take)/gather | solution.py:29
  130.1 0.1 fusion.21
  130.1 0.0 collective-permute-done.1
  130.2 0.9 copy.36
  131.1 0.0 collective-permute-done
  131.1 1.7 copy.34
  132.7 10.5 %maximum_convert_fusion = f32[2,262,3,2048]{1,3,0,2:T(8,128)} fusion(bf16[2,256,3,2048]{1,3,0,2:T(8,128)(2,1)} %copy-done.2, bf16[1,6,3,2048]{1,3,0,2:T(8,128)(2,1)S(1)} %bitcast.68, bf16[1,6,3,2048]{1,3,0,2:T(8,128)(2,1)S(1)} %bitcast.69), kind=kLoop, calls=%fused_computation.16 | loop fusion | flops 19316736 | bytes 19316736 | tf_op jit(solution)/shard_map/convert_element_type | solution.py:45
  143.2 46.7 %fusion = f32[2,256,3,2048]{1,3,0,2:T(8,128)} fusion(f32[2,262,3,2048]{1,3,0,2:T(8,128)} %maximum_convert_fusion, f32[3,2048]{1,0:T(4,128)S(1)} %get-tuple-element.18, f32[3,2048]{1,0:T(4,128)S(1)} %get-tuple-element.19, f32[3,2048]{1,0:T(4,128)S(1)} %get-tuple-element.20, f32[3,2048]{1,0:T(4,128)S(1)} %get-tuple-element.21, ...), kind=kLoop, calls=%fused_computation.4 | loop fusion | flops 40894464 | bytes 100835328 | tf_op jit(solution)/shard_map/add | solution.py:50
  189.8 3.9 fusion.14
  193.8 1.4 copy-done.4
  195.2 1.3 slice_bitcast_fusion.6
  196.5 1.3 collective-permute-start.3
  197.8 4.9 %collective-permute-start.2 = (bf16[127,2048]{0,1:T(8,128)(2,1)}, bf16[127,2048]{0,1:T(8,128)(2,1)S(1)}, u32[]{:S(2)}, u32[]{:S(2)}) collective-permute-start(bf16[127,2048]{0,1:T(8,128)(2,1)} %get-tuple-element.9), channel_id=1, source_target_pairs={{0,2},{2,4},{4,6},{6,8},{8,10},{10,12},{12,14},{14,16},{16,18},{18... | collective-permute-start | bytes 1560584 | tf_op jit(solution)/shard_map/ppermute | solution.py:13
  202.7 13.6 %select_bitcast_fusion = bf16[128,128,255,1,1]{0,2,1,4,3:T(8,128)(2,1)} fusion(bf16[128,255,128]{2,1,0:T(8,128)(2,1)} %reshape.197, pred[128,255]{1,0:T(8,128)(4,1)S(1)} %get-tuple-element.24, pred[128,255]{1,0:T(8,128)(4,1)S(1)} %get-tuple-element.25), kind=kLoop, calls=%fused_computation.17 | loop fusion | flops 8355840 | bytes 16776960 | tf_op jit(solution)/shard_map/jit(_where)/select_n | solution.py:30
  216.3 12.7 %copy.41 = bf16[128,128,255,1,1]{2,1,4,3,0:T(8,128)(2,1)} copy(bf16[128,128,255,1,1]{0,2,1,4,3:T(8,128)(2,1)} %select_bitcast_fusion) | data formatting | bytes 16711680 | tf_op jit(solution)/shard_map/jit(_where)/select_n | solution.py:30
  229.0 0.0 collective-permute-done.3
  229.0 0.0 collective-permute-done.2
  229.0 6.0 %pad_maximum_fusion.1 = (bf16[2,255,2048]{1,2,0:T(8,128)(2,1)}, bf16[2,255,2048]{1,2,0:T(8,128)(2,1)}) fusion(bf16[2,256,2048]{1,2,0:T(8,128)(2,1)} %copy-done.4, bf16[1,127,2048]{1,2,0:T(8,128)(2,1)S(1)} %bitcast.70, bf16[1,127,2048]{1,2,0:T(8,128)(2,1)S(1)} %bitcast.71), kind=kLoop, calls=%fused_computation.30 | loop fusion | flops 6266880 | bytes 9412608 | tf_op jit(solution)/shard_map/concatenate | solution.py:54
  235.0 7.2 %fusion.11 = f32[2,2,128,128,16]{2,4,1,0,3:T(8,128)} fusion(bf16[128,128,255,1,1]{2,1,4,3,0:T(8,128)(2,1)S(1)} %copy-done.3, bf16[2,1,255,128,16]{2,4,3,0,1:T(8,128)(2,1)} %bitcast.67, bf16[2,1,255,128,16]{2,4,3,0,1:T(8,128)(2,1)} %bitcast.66), kind=kOutput, calls=%fused_computation.28 | convolution fusion | flops 536862720 | bytes 16728064 | tf_op jit(solution)/shard_map/grw,snwgc->snrgc/dot_general | solution.py:65
  242.3 6.4 %copy.40 = f32[2,2,128,128,16]{2,1,4,3,0:T(2,128)} copy(f32[2,2,128,128,16]{2,4,1,0,3:T(8,128)} %fusion.11) | data formatting | bytes 8388608 | tf_op jit(solution)/shard_map/grw,snwgc->snrgc/transpose | solution.py:65
  248.7 6.4 %reshape.178 = f32[2,256,2048]{1,2,0:T(8,128)} reshape(f32[2,2,128,128,16]{2,1,4,3,0:T(2,128)} %copy.40) | data formatting | bytes 8388608 | tf_op jit(solution)/shard_map/reshape | solution.py:66
  255.1 6.3 %fusion.8 = bf16[2,256,2048]{1,2,0:T(8,128)(2,1)S(1)} fusion(f32[2,256,3,2048]{1,3,0,2:T(8,128)} %fusion, f32[2,256,2048]{1,2,0:T(8,128)} %reshape.178, f32[2048]{0:T(1024)S(1)} %copy-done.7), kind=kLoop, calls=%fused_computation.23 | loop fusion | flops 7340032 | bytes 18882560 | tf_op jit(solution)/shard_map/convert_element_type | solution.py:67
  261.4 1.0 slice_bitcast_fusion.3
  262.5 13.7 %rev.9 = bf16[256,2048]{0,1:T(8,128)(2,1)S(1)} reverse(bf16[256,2048]{0,1:T(8,128)(2,1)} %slice_bitcast_fusion.3), dimensions={0} | reverse | bytes 2097152 | tf_op jit(solution)/shard_map/jit(_flip)/rev | solution.py:70
  276.2 1.3 fusion.16
  277.5 0.0 all-gather.3.cloned.1.call-update
  277.5 0.0 all-gather.5.cloned.1.call-start
  277.5 0.7 all-gather.5.cloned.1.call-update
  278.2 35.9 %all-gather.3.cloned.1.call-done = bf16[256,4096]{0,1:T(8,128)(2,1)} async-done(((bf16[256,2048]{0,1:T(8,128)(2,1)}), bf16[256,4096]{0,1:T(8,128)(2,1)}) %all-gather.3.cloned.1.call-update) | async-done | bytes 2097168 | tf_op jit(solution)/shard_map/all_gather | solution.py:72
  314.1 129.1 %all-gather.5.cloned.1.call-done = bf16[4096,2048]{1,0:T(8,128)(2,1)} async-done(((bf16[256,2048]{1,0:T(8,128)(2,1)}), bf16[4096,2048]{1,0:T(8,128)(2,1)}) %all-gather.5.cloned.1.call-update) | async-done | bytes 16777232 | tf_op jit(solution)/shard_map/all_gather | solution.py:73
  443.2 11.9 %convolution_convert_fusion = bf16[256,2048]{1,0:T(8,128)(2,1)} fusion(bf16[256,4096]{0,1:T(8,128)(2,1)} %all-gather.3.cloned.1.call-done, bf16[4096,2048]{1,0:T(8,128)(2,1)} %all-gather.5.cloned.1.call-done), kind=kOutput, calls=%fused_computation.27 | convolution fusion | flops 4295491584 | bytes 19922944 | tf_op jit(solution)/shard_map/dot_general | solution.py:74
  (24 shorter events, 0.3 us)
Async XLA Ops:
  6.5 47.8 %copy-start = (bf16[128,128]{1,0:T(8,128)(2,1)S(1)}, bf16[128,128]{1,0:T(8,128)(2,1)}, u32[]{:S(2)}) copy-start(bf16[128,128]{1,0:T(8,128)(2,1)} %param.11) | copy-start | bytes 98308
  6.5 307.6 %all-gather.3.cloned.1.call-start = ((), (), s32[]{:S(2)}) async-start(), calls=%async_computation | async-start | bytes 3145728 | tf_op jit(solution)/shard_map/all_gather | solution.py:72
  27.3 13.0 %copy-start.6 = (s32[256]{0:T(256)S(1)}, s32[256]{0:T(256)}, u32[]{:S(2)}) copy-start(s32[256]{0:T(256)} %param.8) | copy-start | bytes 3076
  43.7 2.6 copy-start.2
  46.4 7.4 %copy-start.5 = (f32[3,7,2048]{2,1,0:T(8,128)S(1)}, f32[3,7,2048]{2,1,0:T(8,128)}, u32[]{:S(2)}) copy-start(f32[3,7,2048]{2,1,0:T(8,128)} %param.10) | copy-start | bytes 516100
  48.0 82.1 %collective-permute-start.1 = (bf16[6,3,2048]{2,0,1:T(8,128)(2,1)S(1)}, bf16[6,3,2048]{2,0,1:T(8,128)(2,1)S(1)}, u32[]{:S(2)}, u32[]{:S(2)}) collective-permute-start(bf16[6,3,2048]{2,0,1:T(8,128)(2,1)S(1)} %copy.35), channel_id=1, source_target_pairs={{2,0},{4,2},{6,4},{8,6},{10,8},{12,10},{14,12},{16,14},{18,16},{20... | collective-permute-start | bytes 221192 | tf_op jit(solution)/shard_map/ppermute | solution.py:13
  50.0 81.0 %collective-permute-start = (bf16[6,3,2048]{2,0,1:T(8,128)(2,1)S(1)}, bf16[6,3,2048]{2,0,1:T(8,128)(2,1)}, u32[]{:S(2)}, u32[]{:S(2)}) collective-permute-start(bf16[6,3,2048]{2,0,1:T(8,128)(2,1)S(1)} %copy.33), channel_id=1, source_target_pairs={{0,2},{2,4},{4,6},{6,8},{8,10},{10,12},{12,14},{14,16},{16,18},{18... | collective-permute-start | bytes 221192 | tf_op jit(solution)/shard_map/ppermute | solution.py:13
  193.8 1.4 copy-start.4
  196.5 32.5 %collective-permute-start.3 = (bf16[127,2048]{0,1:T(8,128)(2,1)}, bf16[127,2048]{0,1:T(8,128)(2,1)S(1)}, u32[]{:S(2)}, u32[]{:S(2)}) collective-permute-start(bf16[127,2048]{0,1:T(8,128)(2,1)} %get-tuple-element.10), channel_id=1, source_target_pairs={{2,0},{4,2},{6,4},{8,6},{10,8},{12,10},{14,12},{16,14},{18,16},{20... | collective-permute-start | bytes 1560584 | tf_op jit(solution)/shard_map/ppermute | solution.py:13
  197.8 31.2 %collective-permute-start.2 = (bf16[127,2048]{0,1:T(8,128)(2,1)}, bf16[127,2048]{0,1:T(8,128)(2,1)S(1)}, u32[]{:S(2)}, u32[]{:S(2)}) collective-permute-start(bf16[127,2048]{0,1:T(8,128)(2,1)} %get-tuple-element.9), channel_id=1, source_target_pairs={{0,2},{2,4},{4,6},{6,8},{8,10},{10,12},{12,14},{14,16},{16,18},{18... | collective-permute-start | bytes 1560584 | tf_op jit(solution)/shard_map/ppermute | solution.py:13
  229.0 6.0 %copy-start.3 = (bf16[128,128,255,1,1]{2,1,4,3,0:T(8,128)(2,1)S(1)}, bf16[128,128,255,1,1]{2,1,4,3,0:T(8,128)(2,1)}, u32[]{:S(2)}) copy-start(bf16[128,128,255,1,1]{2,1,4,3,0:T(8,128)(2,1)} %copy.41) | copy-start | bytes 25067524
  248.7 6.4 %copy-start.7 = (f32[2048]{0:T(1024)S(1)}, f32[2048]{0:T(1024)}, u32[]{:S(2)}) copy-start(f32[2048]{0:T(1024)} %param.12) | copy-start | bytes 24580
  277.5 165.7 %all-gather.5.cloned.1.call-start = ((), (), s32[]{:S(2)}) async-start(), calls=%async_computation.1 | async-start | bytes 17825792 | tf_op jit(solution)/shard_map/all_gather | solution.py:73
  443.2 11.9 %copy-start.1 = (bf16[128,128]{1,0:T(8,128)(2,1)S(1)}, bf16[128,128]{1,0:T(8,128)(2,1)}, u32[]{:S(2)}) copy-start(bf16[128,128]{1,0:T(8,128)(2,1)} %param.11) | copy-start | bytes 98308
Sparse Core Ops, SparseCore 0:
  277.6 36.4 all-gather.2
  316.3 126.8 all-gather.4
where the time goes:
time: 465 us; the launch traced here: 462 us
  waiting for transfers between devices  166 us (36%)
  local copies, waits for them, and re-layouts  159 us (34%)
  other arithmetic  93.2 us (20%)
  matrix products  19.1 us (4%)
  between operations  13.6 us (3%)
  starting transfers between devices  11.2 us (2%)
    all_gather x1, waiting for transfers between devices, per_device(): weight_rows = lax.all_gather(out_weight, 'seq', axis=0, tiled=True)  129 us
    gather x2, local copies, waits for them, and re-layouts, toeplitz(): picked = jnp.take(filters, jnp.clip(tap_index, 0, tap_count - 1), axis=0)  75.7 us
    add x1, other arithmetic, per_device(): short_out + short_filter[:, shift_index, :] * extended[:, begin:begin + l...  46.7 us
    all_gather x1, waiting for transfers between devices, per_device(): gathered = lax.all_gather(averaged, 'ch', axis=1, tiled=True)  35.9 us
    gather x2, local copies, waits for them, and re-layouts, per_device(): features = jnp.take(corner, strand_bases, axis=0)  30.1 us
    rev x1, local copies, waits for them, and re-layouts, per_device(): jnp.flip(reverse, 0).astype(jnp.float32)  13.7 us
    select_n x1, other arithmetic, toeplitz(): jnp.where(inside[:, :, None], picked, jnp.zeros((), filters.dtype))  13.6 us
    select_n x1, local copies, waits for them, and re-layouts, toeplitz(): jnp.where(inside[:, :, None], picked, jnp.zeros((), filters.dtype))  12.7 us
  transfers between devices with their start and end apart: 6, of which 2 were waited for; matrix products, arithmetic and copies ran while one was open for 23% of the time, Pallas kernels for 0%

commit v1 on v0

--- a/solution.py
+++ b/solution.py
@@ -70,7 +70,21 @@
         0.5 * (hidden[0].astype(jnp.float32) + jnp.flip(reverse, 0).astype(jnp.float32))
     ).astype(jnp.bfloat16)
     gathered = lax.all_gather(averaged, "ch", axis=1, tiled=True)
-    weight_rows = lax.all_gather(out_weight, "seq", axis=0, tiled=True)
+    ways, here, step = (lax.axis_size("seq"), lax.axis_index("seq"), out_weight.shape[0])
+    dims = [n * ways if d == 0 else n for d, n in enumerate(out_weight.shape)]
+    full = lax.dynamic_update_slice_in_dim(
+        jnp.zeros(dims, out_weight.dtype), out_weight, here * step, axis=0
+    )
+    going_up = going_down = out_weight
+    for far in range(1, ways // 2 + 1):
+        going_up = lax.ppermute(going_up, "seq", [(d, (d + 1) % ways) for d in range(ways)])
+        full = lax.dynamic_update_slice_in_dim(full, going_up, (here - far) % ways * step, axis=0)
+        if 2 * far < ways:
+            going_down = lax.ppermute(going_down, "seq", [(d, (d - 1) % ways) for d in range(ways)])
+            full = lax.dynamic_update_slice_in_dim(
+                full, going_down, (here + far) % ways * step, axis=0
+            )
+    weight_rows = full
     result = jnp.dot(gathered, weight_rows, preferred_element_type=jnp.float32)
     return result.astype(jnp.bfloat16)
 

time: 465 us -> 413 us (0.89)
  the two profiles are of different devices: /device:TPU:0 before, /device:TPU:6 now
where the time goes in v1:
time: 413 us; the launch traced here: 410 us
  local copies, waits for them, and re-layouts  193 us (47%)
  other arithmetic  91.8 us (22%)
  waiting for transfers between devices  68.6 us (17%)
  starting transfers between devices  23.8 us (6%)
  matrix products  18.9 us (5%)
  between operations  13.9 us (3%)
    gather x2, local copies, waits for them, and re-layouts, toeplitz(): picked = jnp.take(filters, jnp.clip(tap_index, 0, tap_count - 1), axis=0)  75.7 us
    add x1, other arithmetic, per_device(): short_out + short_filter[:, shift_index, :] * extended[:, begin:begin + l...  46.7 us
    ppermute x7, waiting for transfers between devices, per_device(): lax.ppermute(going_down, 'seq', [(d, (d - 1) % ways) for d in range(ways)])  35.4 us
    ppermute x8, waiting for transfers between devices, per_device(): lax.ppermute(going_up, 'seq', [(d, (d + 1) % ways) for d in range(ways)])  33.2 us
    gather x2, local copies, waits for them, and re-layouts, per_device(): features = jnp.take(corner, strand_bases, axis=0)  30.1 us
    dynamic_update_slice x8, local copies, waits for them, and re-layouts, per_device(): lax.dynamic_update_slice_in_dim(full, going_up, (here - far) % ways * ste...  16 us
    dynamic_update_slice x7, local copies, waits for them, and re-layouts, per_device(): lax.dynamic_update_slice_in_dim(full, going_down, (here + far) % ways * s...  13.8 us
    select_n x1, other arithmetic, toeplitz(): jnp.where(inside[:, :, None], picked, jnp.zeros((), filters.dtype))  13.8 us
  transfers between devices with their start and end apart: 20, of which 8 were waited for; matrix products, arithmetic and copies ran while one was open for 70% of the time, Pallas kernels for 0%

profile of v1, /device:TPU:6, one launch (start us, length us, event | category | flops | bytes accessed | tf_op | source)
XLA Modules:
  0.0 409.5 jit_solution(5369000338842051934)
XLA Ops:
  6.5 1.7 collective-permute-start.5
  12.0 17.1 %gather_fusion.1 = bf16[512,3,2048]{2,1,0:T(4,128)(2,1)} fusion(bf16[4,3,2048]{2,1,0:T(4,128)(2,1)S(1)} %copy.31, s32[1024]{0:T(1024)S(1)} %pad_clamp_fusion.1), kind=kCustom, calls=%fused_computation.1 | custom fusion | bytes 12584960 | tf_op jit(solution)/shard_map/jit(_take)/gather | solution.py:43
  29.1 13.0 %copy.32 = bf16[2,256,3,2048]{1,3,0,2:T(8,128)(2,1)} copy(bf16[2,256,3,2048]{3,2,1,0:T(4,128)(2,1)} %bitcast.65) | data formatting | bytes 12582912 | tf_op jit(solution)/shard_map/jit(_take)/gather | solution.py:43
  42.1 3.4 broadcast_select_fusion
  45.5 2.6 copy-done.2
  49.8 1.9 collective-permute-start.1
  52.5 2.6 collective-permute-start
  55.7 65.9 %gather_fusion.2 = bf16[32640,128]{1,0:T(8,128)(2,1)} fusion(bf16[128,128]{1,0:T(8,128)(2,1)S(1)} %copy-done, s32[32768]{0:T(1024)S(1)} %pad_clamp_fusion), kind=kCustom, calls=%fused_computation.2 | custom fusion | bytes 16842240 | tf_op jit(solution)/shard_map/jit(_take)/gather | solution.py:29
  121.6 9.8 %reshape.197 = bf16[128,255,128]{2,1,0:T(8,128)(2,1)} reshape(bf16[32640,128]{1,0:T(8,128)(2,1)} %gather_fusion.2) | data formatting | bytes 16711680 | tf_op jit(solution)/shard_map/jit(_take)/gather | solution.py:29
  134.1 10.4 %maximum_convert_fusion = f32[2,262,3,2048]{1,3,0,2:T(8,128)} fusion(bf16[2,256,3,2048]{1,3,0,2:T(8,128)(2,1)} %copy-done.2, bf16[1,6,3,2048]{1,3,0,2:T(8,128)(2,1)S(1)} %bitcast.68, bf16[1,6,3,2048]{1,3,0,2:T(8,128)(2,1)S(1)} %bitcast.69), kind=kLoop, calls=%fused_computation.16 | loop fusion | flops 19316736 | bytes 19316736 | tf_op jit(solution)/shard_map/convert_element_type | solution.py:45
  144.5 46.7 %fusion = f32[2,256,3,2048]{1,3,0,2:T(8,128)} fusion(f32[2,262,3,2048]{1,3,0,2:T(8,128)} %maximum_convert_fusion, f32[3,2048]{1,0:T(4,128)S(1)} %get-tuple-element.18, f32[3,2048]{1,0:T(4,128)S(1)} %get-tuple-element.19, f32[3,2048]{1,0:T(4,128)S(1)} %get-tuple-element.20, f32[3,2048]{1,0:T(4,128)S(1)} %get-tuple-element.21, ...), kind=kLoop, calls=%fused_computation.4 | loop fusion | flops 40894464 | bytes 100835328 | tf_op jit(solution)/shard_map/add | solution.py:50
  191.2 2.1 collective-permute-start.6
  193.3 3.9 fusion.14
  198.5 2.7 collective-permute-start.3
  201.2 1.9 collective-permute-start.2
  203.2 1.8 collective-permute-start.7
  205.0 18.7 %collective-permute-done.6 = bf16[256,2048]{1,0:T(8,128)(2,1)S(1)} collective-permute-done((bf16[256,2048]{1,0:T(8,128)(2,1)}, bf16[256,2048]{1,0:T(8,128)(2,1)S(1)}, u32[]{:S(2)}, u32[]{:S(2)}) %collective-permute-start.6) | collective-permute-done | bytes 1048608 | tf_op jit(solution)/shard_map/ppermute | solution.py:80
  223.6 13.8 %select_bitcast_fusion = bf16[128,128,255,1,1]{0,2,1,4,3:T(8,128)(2,1)} fusion(bf16[128,255,128]{2,1,0:T(8,128)(2,1)} %reshape.197, pred[128,255]{1,0:T(8,128)(4,1)S(1)} %get-tuple-element.24, pred[128,255]{1,0:T(8,128)(4,1)S(1)} %get-tuple-element.25), kind=kLoop, calls=%fused_computation.17 | loop fusion | flops 8355840 | bytes 16776960 | tf_op jit(solution)/shard_map/jit(_where)/select_n | solution.py:30
  237.8 12.6 %copy.41 = bf16[128,128,255,1,1]{2,1,4,3,0:T(8,128)(2,1)} copy(bf16[128,128,255,1,1]{0,2,1,4,3:T(8,128)(2,1)} %select_bitcast_fusion) | data formatting | bytes 16711680 | tf_op jit(solution)/shard_map/jit(_where)/select_n | solution.py:30
  250.4 6.0 %broadcast_in_dim.49 = bf16[4096,2048]{1,0:T(8,128)(2,1)} broadcast(bf16[]{:T(256)} %constant.136.clone.1), dimensions={} | broadcast | bytes 16777218 | tf_op jit(solution)/shard_map/broadcast_in_dim | solution.py:76
  259.0 4.4 %pad_maximum_fusion.1 = (bf16[2,255,2048]{1,2,0:T(8,128)(2,1)S(1)}, bf16[2,255,2048]{1,2,0:T(8,128)(2,1)}) fusion(bf16[2,256,2048]{1,2,0:T(8,128)(2,1)S(1)} %fusion.14, bf16[1,127,2048]{1,2,0:T(8,128)(2,1)} %bitcast.15, bf16[1,127,2048]{1,2,0:T(8,128)(2,1)} %bitcast.13), kind=kLoop, calls=%fused_computation.30 | loop fusion | flops 6266880 | bytes 9412608 | tf_op jit(solution)/shard_map/concatenate | solution.py:54
  263.4 7.1 %fusion.11 = f32[2,2,128,128,16]{2,4,1,0,3:T(8,128)S(1)} fusion(bf16[128,128,255,1,1]{2,1,4,3,0:T(8,128)(2,1)} %copy.41, bf16[2,1,255,128,16]{2,4,3,0,1:T(8,128)(2,1)} %bitcast.67, bf16[2,1,255,128,16]{2,4,3,0,1:T(8,128)(2,1)S(1)} %bitcast.66), kind=kOutput, calls=%fused_computation.28 | convolution fusion | flops 536862720 | bytes 16728064 | tf_op jit(solution)/shard_map/grw,snwgc->snrgc/dot_general | solution.py:65
  270.4 4.2 %copy.40 = f32[2,2,128,128,16]{2,1,4,3,0:T(2,128)} copy(f32[2,2,128,128,16]{2,4,1,0,3:T(8,128)S(1)} %fusion.11) | data formatting | bytes 8388608 | tf_op jit(solution)/shard_map/grw,snwgc->snrgc/transpose | solution.py:65
  274.6 6.4 %reshape.178 = f32[2,256,2048]{1,2,0:T(8,128)} reshape(f32[2,2,128,128,16]{2,1,4,3,0:T(2,128)} %copy.40) | data formatting | bytes 8388608 | tf_op jit(solution)/shard_map/reshape | solution.py:66
  281.1 1.8 collective-permute-done.9
  282.8 1.9 collective-permute-start.11
  284.7 6.3 %fusion.8 = bf16[2,256,2048]{1,2,0:T(8,128)(2,1)S(1)} fusion(f32[2,256,3,2048]{1,3,0,2:T(8,128)} %fusion, f32[2,256,2048]{1,2,0:T(8,128)} %reshape.178, f32[2048]{0:T(1024)S(1)} %copy-done.7), kind=kLoop, calls=%fused_computation.23 | loop fusion | flops 7340032 | bytes 18882560 | tf_op jit(solution)/shard_map/convert_element_type | solution.py:67
  292.1 13.7 %rev.9 = bf16[256,2048]{0,1:T(8,128)(2,1)S(1)} reverse(bf16[256,2048]{0,1:T(8,128)(2,1)} %slice_bitcast_fusion.3), dimensions={0} | reverse | bytes 2097152 | tf_op jit(solution)/shard_map/jit(_flip)/rev | solution.py:70
  305.8 2.8 collective-permute-done.11
  308.6 1.9 collective-permute-start.13
  311.8 2.3 constant_dynamic-update-slice_fusion.14
  314.1 2.3 constant_dynamic-update-slice_fusion.13
  316.4 2.3 constant_dynamic-update-slice_fusion.12
  318.8 26.8 %collective-permute-done.13 = bf16[256,2048]{1,0:T(8,128)(2,1)} collective-permute-done((bf16[256,2048]{1,0:T(8,128)(2,1)}, bf16[256,2048]{1,0:T(8,128)(2,1)}, u32[]{:S(2)}, u32[]{:S(2)}) %collective-permute-start.13) | collective-permute-done | bytes 1048608 | tf_op jit(solution)/shard_map/ppermute | solution.py:83
  345.6 1.9 collective-permute-start.15
  347.5 2.4 constant_dynamic-update-slice_fusion.11
  349.9 2.3 constant_dynamic-update-slice_fusion.10
  352.2 2.3 constant_dynamic-update-slice_fusion.9
  354.5 2.3 constant_dynamic-update-slice_fusion.8
  356.8 2.3 constant_dynamic-update-slice_fusion.7
  360.1 1.8 collective-permute-start.17
  361.9 2.3 constant_dynamic-update-slice_fusion.6
  364.3 11.3 %collective-permute-done.16 = bf16[256,2048]{1,0:T(8,128)(2,1)S(1)} collective-permute-done((bf16[256,2048]{1,0:T(8,128)(2,1)}, bf16[256,2048]{1,0:T(8,128)(2,1)S(1)}, u32[]{:S(2)}, u32[]{:S(2)}) %collective-permute-start.16) | collective-permute-done | bytes 1048608 | tf_op jit(solution)/shard_map/ppermute | solution.py:80
  375.5 2.4 constant_dynamic-update-slice_fusion.5
  378.0 2.3 constant_dynamic-update-slice_fusion.4
  382.4 3.1 collective-permute-done.17
  386.6 3.2 collective-permute-done.18
  390.8 11.9 %convolution_convert_fusion = bf16[256,2048]{1,0:T(8,128)(2,1)} fusion(bf16[256,4096]{0,1:T(8,128)(2,1)} %all-gather.2.cloned.1.call-done, bf16[4096,2048]{1,0:T(8,128)(2,1)} %constant_dynamic-update-slice_fusion), kind=kOutput, calls=%fused_computation.27 | convolution fusion | flops 4295491584 | bytes 19922944 | tf_op jit(solution)/shard_map/dot_general | solution.py:88
  (68 shorter events, 20.9 us)
Async XLA Ops:
  6.5 49.1 %copy-start = (bf16[128,128]{1,0:T(8,128)(2,1)S(1)}, bf16[128,128]{1,0:T(8,128)(2,1)}, u32[]{:S(2)}) copy-start(bf16[128,128]{1,0:T(8,128)(2,1)} %param.11) | copy-start | bytes 98308
  6.5 384.3 %all-gather.2.cloned.1.call-start = ((), (), s32[]{:S(2)}) async-start(), calls=%async_computation | async-start | bytes 3145728 | tf_op jit(solution)/shard_map/all_gather | solution.py:72
  6.5 184.7 %collective-permute-start.4 = (bf16[256,2048]{1,0:T(8,128)(2,1)}, bf16[256,2048]{1,0:T(8,128)(2,1)}, u32[]{:S(2)}, u32[]{:S(2)}) collective-permute-start(bf16[256,2048]{1,0:T(8,128)(2,1)} %param.13), channel_id=1, source_target_pairs={{0,2},{2,4},{4,6},{6,8},{8,10},{10,12},{12,14},{14,16},{16,18},{18... | collective-permute-start | bytes 3145736 | tf_op jit(solution)/shard_map/ppermute | solution.py:80
  6.5 196.6 %collective-permute-start.5 = (bf16[256,2048]{1,0:T(8,128)(2,1)}, bf16[256,2048]{1,0:T(8,128)(2,1)}, u32[]{:S(2)}, u32[]{:S(2)}) collective-permute-start(bf16[256,2048]{1,0:T(8,128)(2,1)} %param.13), channel_id=1, source_target_pairs={{0,30},{2,0},{4,2},{6,4},{8,6},{10,8},{12,10},{14,12},{16,14},{18,... | collective-permute-start | bytes 3145736 | tf_op jit(solution)/shard_map/ppermute | solution.py:83
  29.1 13.0 %copy-start.6 = (s32[256]{0:T(256)S(1)}, s32[256]{0:T(256)}, u32[]{:S(2)}) copy-start(s32[256]{0:T(256)} %param.8) | copy-start | bytes 3076
  42.1 13.0 %copy-start.5 = (f32[3,7,2048]{2,1,0:T(8,128)S(1)}, f32[3,7,2048]{2,1,0:T(8,128)}, u32[]{:S(2)}) copy-start(f32[3,7,2048]{2,1,0:T(8,128)} %param.10) | copy-start | bytes 516100
  45.5 2.7 copy-start.2
  49.8 81.7 %collective-permute-start.1 = (bf16[6,3,2048]{2,0,1:T(8,128)(2,1)S(1)}, bf16[6,3,2048]{2,0,1:T(8,128)(2,1)S(1)}, u32[]{:S(2)}, u32[]{:S(2)}) collective-permute-start(bf16[6,3,2048]{2,0,1:T(8,128)(2,1)S(1)} %copy.35), channel_id=1, source_target_pairs={{2,0},{4,2},{6,4},{8,6},{10,8},{12,10},{14,12},{16,14},{18,16},{20... | collective-permute-start | bytes 221192 | tf_op jit(solution)/shard_map/ppermute | solution.py:13
  52.5 79.9 %collective-permute-start = (bf16[6,3,2048]{2,0,1:T(8,128)(2,1)S(1)}, bf16[6,3,2048]{2,0,1:T(8,128)(2,1)}, u32[]{:S(2)}, u32[]{:S(2)}) collective-permute-start(bf16[6,3,2048]{2,0,1:T(8,128)(2,1)S(1)} %copy.33), channel_id=1, source_target_pairs={{0,2},{2,4},{4,6},{6,8},{8,10},{10,12},{12,14},{14,16},{16,18},{18... | collective-permute-start | bytes 221192 | tf_op jit(solution)/shard_map/ppermute | solution.py:13
  191.2 32.4 %collective-permute-start.6 = (bf16[256,2048]{1,0:T(8,128)(2,1)}, bf16[256,2048]{1,0:T(8,128)(2,1)S(1)}, u32[]{:S(2)}, u32[]{:S(2)}) collective-permute-start(bf16[256,2048]{1,0:T(8,128)(2,1)} %collective-permute-done.4), channel_id=1, source_target_pairs={{0,2},{2,4},{4,6},{6,8},{8,10},{10,12},{12,14},{14,16},{16,18},{18... | collective-permute-start | bytes 3145736 | tf_op jit(solution)/shard_map/ppermute | solution.py:80
  198.5 60.4 %collective-permute-start.3 = (bf16[127,2048]{0,1:T(8,128)(2,1)}, bf16[127,2048]{0,1:T(8,128)(2,1)}, u32[]{:S(2)}, u32[]{:S(2)}) collective-permute-start(bf16[127,2048]{0,1:T(8,128)(2,1)} %get-tuple-element.10), channel_id=1, source_target_pairs={{2,0},{4,2},{6,4},{8,6},{10,8},{12,10},{14,12},{16,14},{18,16},{20... | collective-permute-start | bytes 1560584 | tf_op jit(solution)/shard_map/ppermute | solution.py:13
  201.2 57.7 %collective-permute-start.2 = (bf16[127,2048]{0,1:T(8,128)(2,1)}, bf16[127,2048]{0,1:T(8,128)(2,1)}, u32[]{:S(2)}, u32[]{:S(2)}) collective-permute-start(bf16[127,2048]{0,1:T(8,128)(2,1)} %get-tuple-element.9), channel_id=1, source_target_pairs={{0,2},{2,4},{4,6},{6,8},{8,10},{10,12},{12,14},{14,16},{16,18},{18... | collective-permute-start | bytes 1560584 | tf_op jit(solution)/shard_map/ppermute | solution.py:13
  203.2 54.3 %collective-permute-start.7 = (bf16[256,2048]{1,0:T(8,128)(2,1)}, bf16[256,2048]{1,0:T(8,128)(2,1)}, u32[]{:S(2)}, u32[]{:S(2)}) collective-permute-start(bf16[256,2048]{1,0:T(8,128)(2,1)} %collective-permute-done.5), channel_id=1, source_target_pairs={{0,30},{2,0},{4,2},{6,4},{8,6},{10,8},{12,10},{14,12},{16,14},{18,... | collective-permute-start | bytes 3145736 | tf_op jit(solution)/shard_map/ppermute | solution.py:83
  223.6 13.9 %copy-start.4 = (bf16[256,2048]{1,0:T(8,128)(2,1)}, bf16[256,2048]{1,0:T(8,128)(2,1)S(1)}, u32[]{:S(2)}) copy-start(bf16[256,2048]{1,0:T(8,128)(2,1)S(1)} %collective-permute-done.6) | copy-start | bytes 3145732
  223.6 35.3 %collective-permute-start.8 = (bf16[256,2048]{1,0:T(8,128)(2,1)S(1)}, bf16[256,2048]{1,0:T(8,128)(2,1)}, u32[]{:S(2)}, u32[]{:S(2)}) collective-permute-start(bf16[256,2048]{1,0:T(8,128)(2,1)S(1)} %collective-permute-done.6), channel_id=1, source_target_pairs={{0,2},{2,4},{4,6},{6,8},{8,10},{10,12},{12,14},{14,16},{16,18},{18... | collective-permute-start | bytes 3145736 | tf_op jit(solution)/shard_map/ppermute | solution.py:80
  250.4 6.0 %copy-start.3 = (bf16[256,2048]{1,0:T(8,128)(2,1)S(1)}, bf16[256,2048]{1,0:T(8,128)(2,1)}, u32[]{:S(2)}) copy-start(bf16[256,2048]{1,0:T(8,128)(2,1)} %param.13) | copy-start | bytes 3145732
  257.5 25.4 %collective-permute-start.9 = (bf16[256,2048]{1,0:T(8,128)(2,1)}, bf16[256,2048]{1,0:T(8,128)(2,1)}, u32[]{:S(2)}, u32[]{:S(2)}) collective-permute-start(bf16[256,2048]{1,0:T(8,128)(2,1)} %collective-permute-done.7), channel_id=1, source_target_pairs={{0,30},{2,0},{4,2},{6,4},{8,6},{10,8},{12,10},{14,12},{16,14},{18,... | collective-permute-start | bytes 3145736 | tf_op jit(solution)/shard_map/ppermute | solution.py:83
  259.0 25.8 %collective-permute-start.10 = (bf16[256,2048]{1,0:T(8,128)(2,1)}, bf16[256,2048]{1,0:T(8,128)(2,1)}, u32[]{:S(2)}, u32[]{:S(2)}) collective-permute-start(bf16[256,2048]{1,0:T(8,128)(2,1)} %collective-permute-done.8), channel_id=1, source_target_pairs={{0,2},{2,4},{4,6},{6,8},{8,10},{10,12},{12,14},{14,16},{16,18},{18... | collective-permute-start | bytes 3145736 | tf_op jit(solution)/shard_map/ppermute | solution.py:80
  270.4 14.3 %copy-start.7 = (f32[2048]{0:T(1024)S(1)}, f32[2048]{0:T(1024)}, u32[]{:S(2)}) copy-start(f32[2048]{0:T(1024)} %param.12) | copy-start | bytes 24580
  282.8 25.8 %collective-permute-start.11 = (bf16[256,2048]{1,0:T(8,128)(2,1)}, bf16[256,2048]{1,0:T(8,128)(2,1)}, u32[]{:S(2)}, u32[]{:S(2)}) collective-permute-start(bf16[256,2048]{1,0:T(8,128)(2,1)} %collective-permute-done.9), channel_id=1, source_target_pairs={{0,30},{2,0},{4,2},{6,4},{8,6},{10,8},{12,10},{14,12},{16,14},{18,... | collective-permute-start | bytes 3145736 | tf_op jit(solution)/shard_map/ppermute | solution.py:83
  284.7 25.8 %collective-permute-start.12 = (bf16[256,2048]{1,0:T(8,128)(2,1)}, bf16[256,2048]{1,0:T(8,128)(2,1)}, u32[]{:S(2)}, u32[]{:S(2)}) collective-permute-start(bf16[256,2048]{1,0:T(8,128)(2,1)} %collective-permute-done.10), channel_id=1, source_target_pairs={{0,2},{2,4},{4,6},{6,8},{8,10},{10,12},{12,14},{14,16},{16,18},{18... | collective-permute-start | bytes 3145736 | tf_op jit(solution)/shard_map/ppermute | solution.py:80
  308.6 37.0 %collective-permute-start.13 = (bf16[256,2048]{1,0:T(8,128)(2,1)}, bf16[256,2048]{1,0:T(8,128)(2,1)}, u32[]{:S(2)}, u32[]{:S(2)}) collective-permute-start(bf16[256,2048]{1,0:T(8,128)(2,1)} %collective-permute-done.11), channel_id=1, source_target_pairs={{0,30},{2,0},{4,2},{6,4},{8,6},{10,8},{12,10},{14,12},{16,14},{18,... | collective-permute-start | bytes 3145736 | tf_op jit(solution)/shard_map/ppermute | solution.py:83
  310.5 39.4 %collective-permute-start.14 = (bf16[256,2048]{1,0:T(8,128)(2,1)}, bf16[256,2048]{1,0:T(8,128)(2,1)}, u32[]{:S(2)}, u32[]{:S(2)}) collective-permute-start(bf16[256,2048]{1,0:T(8,128)(2,1)} %collective-permute-done.12), channel_id=1, source_target_pairs={{0,2},{2,4},{4,6},{6,8},{8,10},{10,12},{12,14},{14,16},{16,18},{18... | collective-permute-start | bytes 3145736 | tf_op jit(solution)/shard_map/ppermute | solution.py:80
  345.6 14.5 %collective-permute-start.15 = (bf16[256,2048]{1,0:T(8,128)(2,1)}, bf16[256,2048]{1,0:T(8,128)(2,1)S(1)}, u32[]{:S(2)}, u32[]{:S(2)}) collective-permute-start(bf16[256,2048]{1,0:T(8,128)(2,1)} %collective-permute-done.13), channel_id=1, source_target_pairs={{0,30},{2,0},{4,2},{6,4},{8,6},{10,8},{12,10},{14,12},{16,14},{18,... | collective-permute-start | bytes 3145736 | tf_op jit(solution)/shard_map/ppermute | solution.py:83
  349.9 25.7 %collective-permute-start.16 = (bf16[256,2048]{1,0:T(8,128)(2,1)}, bf16[256,2048]{1,0:T(8,128)(2,1)S(1)}, u32[]{:S(2)}, u32[]{:S(2)}) collective-permute-start(bf16[256,2048]{1,0:T(8,128)(2,1)} %collective-permute-done.14), channel_id=1, source_target_pairs={{0,2},{2,4},{4,6},{6,8},{8,10},{10,12},{12,14},{14,16},{16,18},{18... | collective-permute-start | bytes 3145736 | tf_op jit(solution)/shard_map/ppermute | solution.py:80
  360.1 25.4 %collective-permute-start.17 = (bf16[256,2048]{1,0:T(8,128)(2,1)S(1)}, bf16[256,2048]{1,0:T(8,128)(2,1)S(1)}, u32[]{:S(2)}, u32[]{:S(2)}) collective-permute-start(bf16[256,2048]{1,0:T(8,128)(2,1)S(1)} %collective-permute-done.15), channel_id=1, source_target_pairs={{0,30},{2,0},{4,2},{6,4},{8,6},{10,8},{12,10},{14,12},{16,14},{18,... | collective-permute-start | bytes 3145736 | tf_op jit(solution)/shard_map/ppermute | solution.py:83
  375.5 14.2 %collective-permute-start.18 = (bf16[256,2048]{1,0:T(8,128)(2,1)S(1)}, bf16[256,2048]{1,0:T(8,128)(2,1)S(1)}, u32[]{:S(2)}, u32[]{:S(2)}) collective-permute-start(bf16[256,2048]{1,0:T(8,128)(2,1)S(1)} %collective-permute-done.16), channel_id=1, source_target_pairs={{0,2},{2,4},{4,6},{6,8},{8,10},{10,12},{12,14},{14,16},{16,18},{18... | collective-permute-start | bytes 3145736 | tf_op jit(solution)/shard_map/ppermute | solution.py:80
  389.8 12.9 %copy-start.1 = (bf16[128,128]{1,0:T(8,128)(2,1)S(1)}, bf16[128,128]{1,0:T(8,128)(2,1)}, u32[]{:S(2)}) copy-start(bf16[128,128]{1,0:T(8,128)(2,1)} %param.11) | copy-start | bytes 98308
Sparse Core Ops, SparseCore 0:
  311.9 31.6 all-gather.1
